TPU v7x, 256 devices: a whole 4x4x8 slice. The times are simulated.
256 devices in a mesh: path: 64 (over y, z, core), inner: 4 (over x).
Axes of the slice: x: 4, y: 4, z: 8, core: 2. Of those that a mesh axis runs over, the one named last changes fastest.
Arguments:
- acts: bfloat16 [65536, 2048], P(('path', 'inner')), may hold values from -6 to 6
- cotan: bfloat16 [65536, 2048], P(('path', 'inner')), may hold values from -6 to 6
- w_in: bfloat16 [64, 2048, 2048], P('path', None, 'inner'), may hold values from -0.125 to 0.125
- w_out_t: bfloat16 [64, 2048, 2048], P('path', None, 'inner'), may hold values from -0.125 to 0.125
- choose: int32 [64, 2], replicated, may hold values from 0 to 7
- momentum: float32 [2, 8, 2048, 2048], P(None, None, 'path', 'inner'), may hold values from -6 to 6
Outputs:
- new_in: bfloat16 [64, 2048, 2048], P('path', None, 'inner')
- new_out_t: bfloat16 [64, 2048, 2048], P('path', None, 'inner')
- new_momentum: float32 [2, 8, 2048, 2048], P(None, None, 'path', 'inner')
All inputs are finite; a program needn't handle non-finite values. Where the computation divides by a largest or mean magnitude, that divisor is 1e-20 or more.
Results may differ from a plain program's by a relative error of at most 0.015.
Values may be sent and summed in bfloat16 or wider, within the bound.
A program may use at most 128 MiB of HBM per device.

v0:
```python
import functools

import jax
import jax.numpy as jnp
from jax import lax
from jax.experimental import pallas as pl
from jax.experimental.pallas import tpu as pltpu
from jax.sharding import PartitionSpec as P

MU = 0.9
OUTER_LR = 0.7
MESH = pl.DeviceIdType.MESH

NX, NY, NZ, NC = 4, 4, 8, 2
GRID = 8
TOK = 256
TOKENS = TOK * NX
D = 2048
COLS = D // NX
PIECE = D // (NY * NZ * NC)
NPAIR = NZ // 2
PAIR = 2 * NC * PIECE
CHUNK = NY * PAIR
PEERS = [(2, 0), (2, 1), (1, 0), (1, 1), (3, 0), (3, 1), (0, 1)]
NP = len(PEERS)
ORDER = [2, 1, 3, 0]
HOPS = [4, 3, 2, 1, -3, -2, -1]


def contract_first(left, right):
    return lax.dot_general(
        left, right, (((0,), (0,)), ((), ())), preferred_element_type=jnp.float32
    )


class Body:
    def __init__(self, ins, outs, scratch):
        self.x_hbm, self.c_hbm, self.w1_hbm, self.w2_hbm, self.ch, self.chv, self.mom_hbm = ins
        self.f_hbm = outs[:2]
        self.nm_hbm = outs[2]
        for name, ref in scratch.items():
            setattr(self, name, ref)
        path = lax.axis_index("path")
        self.x = lax.axis_index("inner")
        self.y = lax.div(path, NZ * NC)
        self.z = lax.rem(lax.div(path, NC), NZ)
        self.c = lax.rem(path, NC)
        self.zp = lax.div(self.z, 2)

    def path_of(self, dy=0, dz=0, dc=0):
        y = lax.rem(self.y + (dy + NY), NY)
        z = lax.rem(self.z + (dz + NZ), NZ)
        c = lax.rem(self.c + (dc + NC), NC)
        return (y * NZ + z) * NC + c

    def dev(self, dy=0, dz=0, dc=0, dx=0):
        return (self.path_of(dy, dz, dc), lax.rem(self.x + (dx + NX), NX))

    def send(self, src, dst, ssem, rsem, dev):
        pltpu.make_async_remote_copy(
            src_ref=src, dst_ref=dst, send_sem=ssem, recv_sem=rsem, device_id=dev, device_id_type=MESH
        ).start()

    def wait(self, ref, sem):
        pltpu.make_async_copy(ref, ref, sem).wait()

    def barrier(self):
        bar = pltpu.get_barrier_semaphore()
        partners = [self.dev(dx=k) for k in (1, 2, 3)]
        partners += [self.dev(dy=dy, dc=dc) for dy, dc in PEERS]
        partners += [self.dev(dz=1), self.dev(dz=-1)]
        for partner in partners:
            pl.semaphore_signal(bar, inc=1, device_id=partner, device_id_type=MESH)
        pl.semaphore_wait(bar, len(partners))

    def pair(self, i):
        return lax.rem(self.zp + ORDER[i], NPAIR)

    def load_local(self):
        for a, (hbm, whbm, wbuf) in enumerate(
            ((self.x_hbm, self.w1_hbm, self.W1), (self.c_hbm, self.w2_hbm, self.W2))
        ):
            for i in range(NPAIR):
                q = self.pair(i)

                def one(yy, _, a=a, i=i, q=q, hbm=hbm, whbm=whbm, wbuf=wbuf):
                    cols = pl.multiple_of(yy * (NPAIR * PAIR) + q * PAIR, PAIR)
                    place = pl.multiple_of(yy * PAIR, PAIR)
                    pltpu.make_async_copy(
                        hbm.at[:, pl.ds(cols, PAIR)],
                        self.T2[a].at[q, pl.ds(pl.multiple_of(self.x * TOK, TOK), TOK), pl.ds(place, PAIR)],
                        self.lsem.at[a, i],
                    ).start()
                    pltpu.make_async_copy(
                        whbm.at[pl.ds(cols, PAIR)], wbuf.at[q, pl.ds(place, PAIR)], self.lsem.at[a, i]
                    ).start()
                    return 0

                lax.fori_loop(0, NY, one, 0)
        pltpu.make_async_copy(self.mom_hbm, self.MOM, self.msem.at[0]).start()

    def send_tokens(self, a, i):
        hbm = (self.x_hbm, self.c_hbm)[a]
        q = self.pair(i)

        def one(yy, _):
            cols = pl.multiple_of(yy * (NPAIR * PAIR) + q * PAIR, PAIR)
            place = pl.multiple_of(yy * PAIR, PAIR)
            for dx in (2, 1, 3):
                self.send(
                    hbm.at[:, pl.ds(cols, PAIR)],
                    self.T2[a].at[q, pl.ds(pl.multiple_of(self.x * TOK, TOK), TOK), pl.ds(place, PAIR)],
                    self.tssem.at[a],
                    self.trsem.at[a, i],
                    self.dev(dx=dx),
                )
            return 0

        lax.fori_loop(0, NY, one, 0)

    def wait_tokens(self, a, i):
        q = self.pair(i)
        wbuf = (self.W1, self.W2)[a]
        self.wait(self.T2[a].at[q, pl.ds(0, TOK)], self.lsem.at[a, i])
        self.wait(wbuf.at[q], self.lsem.at[a, i])
        self.wait(self.T2[a].at[q, pl.ds(0, TOKENS - TOK)], self.trsem.at[a, i])

    def product(self, a, i):
        q = self.pair(i)
        wbuf = (self.W1, self.W2)[a]

        def one(h, _):
            rows = pl.ds(pl.multiple_of(h * 512, 512), 512)
            part = jnp.dot(self.T2[a][q, rows], wbuf[q], preferred_element_type=jnp.float32)
            if i == 0:
                self.ACC[rows] = part
            else:
                self.ACC[rows] = self.ACC[rows] + part
            return 0

        lax.fori_loop(0, TOKENS // 512, one, 0)

    def activate(self):
        def one(h, _):
            rows = pl.ds(pl.multiple_of(h * 64, 64), 64)
            t = jnp.tanh(self.ACC[rows])
            self.TB[rows] = t.astype(jnp.bfloat16)
            self.SL[rows] = 1.0 - t * t
            return 0

        lax.fori_loop(0, TOKENS // 64, one, 0)

    def slope(self):
        def one(h, _):
            rows = pl.ds(pl.multiple_of(h * 64, 64), 64)
            self.DS[rows] = (self.ACC[rows] * self.SL[rows]).astype(jnp.bfloat16)
            return 0

        lax.fori_loop(0, TOKENS // 64, one, 0)

    def gradient(self, level, i):
        q = self.pair(i)
        left = self.T2[level]
        right = (self.DS, self.TB)[level]

        def one(h, _):
            cols = pl.ds(pl.multiple_of(h * 256, 256), 256)
            g = contract_first(left[q, :, cols], right[...]) * (1.0 / TOKENS**0.5)
            self.S[level, q, pl.ds(h * 2, 2)] = g.astype(jnp.bfloat16).reshape(2, 2, NC, PIECE, COLS)
            return 0

        lax.fori_loop(0, CHUNK // 256, one, 0)

    def send_gradient(self, level, i):
        q = self.pair(i)
        for k, (dy, dc) in enumerate(PEERS):
            yy = lax.rem(self.y + dy, NY)
            cc = lax.rem(self.c + dc, NC)
            self.send(
                self.S.at[level, q, yy, :, cc],
                self.R.at[level, k, pl.ds(q * 2, 2)],
                self.yssem.at[level],
                self.yrsem.at[level, i],
                self.dev(dy=dy, dc=dc),
            )

    def wait_gradient(self, level, i):
        q = self.pair(i)
        self.wait(self.R.at[level, :, pl.ds(q * 2, 2)], self.yrsem.at[level, i])

    def passed(self, level, d, use):
        t = lax.rem(self.z + (d + NZ), NZ)
        q = lax.div(t, 2)
        low = lax.rem(t, 2)
        ids = [self.ch[self.path_of() * 2 + level]]
        ids += [self.ch[self.path_of(dy=-dy, dc=-dc) * 2 + level] for dy, dc in PEERS]
        weight = [[jnp.where(i == m, 1.0, 0.0).astype(jnp.float32) for m in range(GRID)] for i in ids]

        def one(b, _):
            cols = pl.ds(pl.multiple_of(b * 128, 128), 128)
            parts = [self.S[level, q, self.y, low, self.c, :, cols].astype(jnp.float32)]
            parts += [self.R[level, k, t, :, cols].astype(jnp.float32) for k in range(NP)]
            for m in range(GRID):
                total = parts[0] * weight[0][m]
                for s in range(1, NP + 1):
                    total = total + parts[s] * weight[s][m]
                use(m, cols, total)
            return 0

        lax.fori_loop(0, COLS // 128, one, 0)

    def hop(self, level, d):
        slot = HOPS.index(d)
        up = d > 0
        came = self.UP if up else self.DOWN
        if d == 4:

            def use(m, cols, total):
                self.SB[level, slot, m, :, cols] = total.astype(jnp.bfloat16)

        else:
            k = abs(d)
            self.wait(self.arriving(level, up, k), (self.usem if up else self.dsem).at[level, k])

            def use(m, cols, total):
                if k < 3 or (m < GRID // 2) == up:
                    total = total + came[level, k, m, :, cols].astype(jnp.float32)
                self.SB[level, slot, m, :, cols] = total.astype(jnp.bfloat16)

        self.passed(level, d, use)
        half = GRID // 2
        if d == 4:
            lo, hi = pl.ds(0, half), pl.ds(half, half)
            self.send(self.SB.at[level, slot, lo], self.UP.at[level, 3, lo], self.zssem.at[level], self.usem.at[level, 3], self.dev(dz=1))
            self.send(self.SB.at[level, slot, hi], self.DOWN.at[level, 3, hi], self.zssem.at[level], self.dsem.at[level, 3], self.dev(dz=-1))
        elif up:
            self.send(self.SB.at[level, slot], self.UP.at[level, d - 1], self.zssem.at[level], self.usem.at[level, d - 1], self.dev(dz=1))
        else:
            self.send(self.SB.at[level, slot], self.DOWN.at[level, -d - 1], self.zssem.at[level], self.dsem.at[level, -d - 1], self.dev(dz=-1))

    def arriving(self, level, up, k):
        half = GRID // 2
        buf = self.UP if up else self.DOWN
        if k == 3:
            return buf.at[level, 3, pl.ds(0 if up else half, half)]
        return buf.at[level, k]

    def counts(self):
        for level in range(2):
            ids = self.chv[:, level : level + 1]
            for m in range(GRID):
                n = jnp.sum(jnp.where(ids == m, 1.0, 0.0), axis=0, keepdims=True)
                self.INV[level, m] = jnp.broadcast_to(1.0 / jnp.maximum(n, 1.0), (8, 128))

    def own(self, level):
        if level == 1:
            self.wait(self.MOM, self.msem.at[0])
        self.wait(self.UP.at[level, 0], self.usem.at[level, 0])
        self.wait(self.DOWN.at[level, 0], self.dsem.at[level, 0])

        def use(m, cols, total):
            total = total + self.UP[level, 0, m, :, cols].astype(jnp.float32)
            total = total + self.DOWN[level, 0, m, :, cols].astype(jnp.float32)
            avg = total * self.INV[level, m, :1]
            mom = MU * self.MOM[level, m, :, cols] + avg
            self.NM[level, m, :, cols] = mom
            self.U[level][0][m, :, cols] = (MU * mom + avg).astype(jnp.bfloat16)

        self.passed(level, 0, use)
        pltpu.make_async_copy(self.NM.at[level], self.nm_hbm.at[level], self.msem.at[1 + level]).start()
        self.spread(level, 0)

    def spread(self, level, d):
        half = GRID // 2
        src = self.U[level][d % NZ]
        if d <= 0:
            to = (d - 1) % NZ
            rows = pl.ds(0, half) if d == -3 else pl.ds(0, GRID)
            self.send(src.at[rows], self.U[level][to].at[rows], self.gssem.at[level], self.gusem.at[level, 1 - d], self.dev(dz=1))
        if d >= 0:
            to = (d + 1) % NZ
            rows = pl.ds(half, half) if d == 3 else pl.ds(0, GRID)
            self.send(src.at[rows], self.U[level][to].at[rows], self.gssem.at[level], self.gdsem.at[level, d + 1], self.dev(dz=-1))

    def wait_spread(self, level, d):
        half = GRID // 2
        buf = self.U[level][d % NZ]
        if d == 4:
            self.wait(buf.at[pl.ds(0, half)], self.gusem.at[level, 4])
            self.wait(buf.at[pl.ds(half, half)], self.gdsem.at[level, 4])
        elif d < 0:
            self.wait(buf, self.gusem.at[level, -d])
        else:
            self.wait(buf, self.gdsem.at[level, d])

    def give(self, level, d):
        t = lax.rem(self.z + (d + NZ), NZ)
        rows = pl.ds(pl.multiple_of((self.y * NZ + t) * (NC * PIECE) + self.c * PIECE, PIECE), PIECE)
        buf = self.U[level][d % NZ]
        dst = self.f_hbm[level].at[rows]
        for k, (dy, dc) in enumerate(PEERS):
            m = self.ch[self.path_of(dy=dy, dc=dc) * 2 + level]
            self.SEL[level, d % NZ, k] = buf[m]
            self.send(self.SEL.at[level, d % NZ, k], dst, self.fssem.at[level], self.frsem.at[level], self.dev(dy=dy, dc=dc))
        m = self.ch[self.path_of() * 2 + level]
        self.SEL[level, d % NZ, NP] = buf[m]
        pltpu.make_async_copy(self.SEL.at[level, d % NZ, NP], dst, self.flsem.at[level]).start()

    def finish(self):
        for level in range(2):
            self.wait(self.f_hbm[level].at[pl.ds(0, D // 8 * 7)], self.frsem.at[level])
            self.wait(self.f_hbm[level].at[pl.ds(0, D // 8)], self.flsem.at[level])
            self.wait(self.SEL.at[level, :, pl.ds(0, NP)], self.fssem.at[level])
            self.wait(self.SB.at[level], self.zssem.at[level])
            self.wait(self.SB.at[level], self.gssem.at[level])
            self.wait(self.R.at[level], self.yssem.at[level])
            self.wait(self.T2[level].at[pl.ds(0, 3)], self.tssem.at[level])
            self.wait(self.NM.at[level], self.msem.at[1 + level])

    def run(self):
        self.load_local()
        self.counts()
        self.barrier()
        for a in (0, 1):
            for i in range(NPAIR):
                self.send_tokens(a, i)
        for i in range(NPAIR):
            self.wait_tokens(0, i)
            self.product(0, i)
        self.activate()
        for i in range(NPAIR):
            self.wait_tokens(1, i)
            self.gradient(1, i)
            self.send_gradient(1, i)
            self.product(1, i)
            if i == 1:
                self.wait_gradient(1, 0)
                self.hop(1, 4)
            if i == 2:
                self.wait_gradient(1, 1)
                self.hop(1, 3)
                self.hop(1, 2)
        self.slope()
        for i in range(NPAIR):
            self.gradient(0, i)
            self.send_gradient(0, i)
        self.wait_gradient(1, 2)
        self.hop(1, -3)
        self.hop(1, -2)
        self.wait_gradient(1, 3)
        self.hop(1, 1)
        self.hop(1, -1)
        self.wait_gradient(0, 0)
        self.hop(0, 4)
        self.own(1)
        self.wait_gradient(0, 1)
        self.hop(0, 3)
        self.hop(0, 2)
        self.give(1, 0)

        def step(level, k):
            for d in (-k, k) if k < 4 else (4,):
                self.wait_spread(level, d)
                if k < 4:
                    self.spread(level, d)
            for d in (-k, k) if k < 4 else (4,):
                self.give(level, d)

        step(1, 1)
        self.wait_gradient(0, 2)
        self.hop(0, -3)
        self.hop(0, -2)
        step(1, 2)
        self.wait_gradient(0, 3)
        self.hop(0, 1)
        self.hop(0, -1)
        step(1, 3)
        self.own(0)
        self.give(0, 0)
        step(1, 4)
        for k in (1, 2, 3, 4):
            step(0, k)
        self.finish()


SCRATCH = dict(
    X=pltpu.VMEM((NPAIR, TOKENS, CHUNK), jnp.bfloat16),
    C=pltpu.VMEM((NPAIR, TOKENS, CHUNK), jnp.bfloat16),
    W1=pltpu.VMEM((NPAIR, CHUNK, COLS), jnp.bfloat16),
    W2=pltpu.VMEM((NPAIR, CHUNK, COLS), jnp.bfloat16),
    ACC=pltpu.VMEM((TOKENS, COLS), jnp.float32),
    SL=pltpu.VMEM((TOKENS, COLS), jnp.float32),
    TB=pltpu.VMEM((TOKENS, COLS), jnp.bfloat16),
    DS=pltpu.VMEM((TOKENS, COLS), jnp.bfloat16),
    S=pltpu.VMEM((2, NPAIR, NY, 2, NC, PIECE, COLS), jnp.bfloat16),
    R=pltpu.VMEM((2, NP, NZ, PIECE, COLS), jnp.bfloat16),
    SB=pltpu.VMEM((2, len(HOPS), GRID, PIECE, COLS), jnp.bfloat16),
    UP=pltpu.VMEM((2, 4, GRID, PIECE, COLS), jnp.bfloat16),
    DOWN=pltpu.VMEM((2, 4, GRID, PIECE, COLS), jnp.bfloat16),
    MOM=pltpu.VMEM((2, GRID, PIECE, COLS), jnp.float32),
    NM=pltpu.VMEM((2, GRID, PIECE, COLS), jnp.float32),
    INV=pltpu.VMEM((2, GRID, 8, 128), jnp.float32),
    SEL=pltpu.VMEM((2, NZ, NP + 1, PIECE, COLS), jnp.bfloat16),
    lsem=pltpu.SemaphoreType.DMA((2, NPAIR)),
    tssem=pltpu.SemaphoreType.DMA((2,)),
    trsem=pltpu.SemaphoreType.DMA((2, NPAIR)),
    yssem=pltpu.SemaphoreType.DMA((2,)),
    yrsem=pltpu.SemaphoreType.DMA((2, NPAIR)),
    zssem=pltpu.SemaphoreType.DMA((2,)),
    usem=pltpu.SemaphoreType.DMA((2, 4)),
    dsem=pltpu.SemaphoreType.DMA((2, 4)),
    gssem=pltpu.SemaphoreType.DMA((2,)),
    gusem=pltpu.SemaphoreType.DMA((2, 5)),
    gdsem=pltpu.SemaphoreType.DMA((2, 5)),
    fssem=pltpu.SemaphoreType.DMA((2,)),
    frsem=pltpu.SemaphoreType.DMA((2,)),
    flsem=pltpu.SemaphoreType.DMA((2,)),
    msem=pltpu.SemaphoreType.DMA((3,)),
)
UPDATES = [pltpu.VMEM((GRID, PIECE, COLS), jnp.bfloat16)] * (2 * NZ)


def kernel(*refs):
    ins, outs, rest = refs[:7], refs[7:10], refs[10:]
    named = dict(zip(SCRATCH, rest))
    body = Body(ins, outs, named)
    updates = rest[len(SCRATCH) :]
    body.U = [updates[:NZ], updates[NZ:]]
    body.T2 = [body.X, body.C]
    body.run()


def sync(acts, cotan, first, second, choose, momentum):
    hbm = pl.BlockSpec(memory_space=pl.ANY)
    return pl.pallas_call(
        kernel,
        out_shape=(
            jax.ShapeDtypeStruct((D, COLS), jnp.bfloat16),
            jax.ShapeDtypeStruct((D, COLS), jnp.bfloat16),
            jax.ShapeDtypeStruct(momentum.shape, jnp.float32),
        ),
        in_specs=[hbm] * 4
        + [pl.BlockSpec(memory_space=pltpu.SMEM), pl.BlockSpec(memory_space=pltpu.VMEM), hbm],
        out_specs=[hbm] * 3,
        scratch_shapes=list(SCRATCH.values()) + UPDATES,
        compiler_params=pltpu.CompilerParams(
            collective_id=0, has_side_effects=True, vmem_limit_bytes=58 * 2**20
        ),
        cost_estimate=pl.CostEstimate(flops=8 * 10**9, bytes_accessed=2 * 10**7, transcendentals=0),
    )(acts, cotan, first, second, choose.reshape(-1), choose, momentum)


def on_device(acts, cotan, w_in, w_out_t, choose, momentum):
    first, second = w_in[0], w_out_t[0]
    update_in, update_out, new_momentum = sync(acts, cotan, first, second, choose, momentum)

    def apply(weight, update):
        return (weight.astype(jnp.float32) - OUTER_LR * update.astype(jnp.float32)).astype(jnp.bfloat16)

    return (apply(first, update_in)[None], apply(second, update_out)[None], new_momentum)


def solution(mesh):
    return jax.shard_map(
        on_device,
        mesh=mesh,
        in_specs=(
            P(("path", "inner"), None),
            P(("path", "inner"), None),
            P("path", None, "inner"),
            P("path", None, "inner"),
            P(),
            P(None, None, "path", "inner"),
        ),
        out_specs=(
            P("path", None, "inner"),
            P("path", None, "inner"),
            P(None, None, "path", "inner"),
        ),
        check_vma=False,
    )
```

profile of v0, /device:TPU:1, one launch (start us, length us, event | category | flops | bytes accessed | tf_op | source)
XLA Modules:
  0.0 215.9 jit_solution(3479704371995388186)
XLA Ops:
  0.6 0.8 copy.11.refs_5_
  1.4 0.0 copy-start.3
  1.4 0.7 reshape.9.refs_4_
  2.1 0.0 copy-done.3
  2.1 0.0 copy-start
  2.1 0.0 copy-start.1
  2.1 207.3 %shard_map.85 = (bf16[2048,512]{1,0:T(8,128)(2,1)}, bf16[2048,512]{1,0:T(8,128)(2,1)}, f32[2,8,32,512]{3,2,1,0:T(8,128)}) custom-call(bf16[256,2048]{1,0:T(8,128)(2,1)} %refs_0_.1, bf16[256,2048]{1,0:T(8,128)(2,1)} %refs_1_.1, bf16[2048,512]{1,0:T(8,128)(2,1)} %bitcast.8, bf16[2048,512]{1,0:T(8,128)(2,1)} %bitcast.9, s32[128]{0:T(128)} %reshape.9.refs_4_, ...), custom_call_target="tpu_custom_call" | custom-call | flops 8000000000 | bytes 20000000 | tf_op jit(solution)/shard_map/pallas_call | solution.py:435
  209.3 0.0 copy-done
  209.3 0.0 copy-done.1
  209.4 0.0 copy-start.2
  209.4 5.6 %fusion = (bf16[1,2048,512]{2,1,0:T(8,128)(2,1)}, bf16[1,2048,512]{2,1,0:T(8,128)(2,1)}) fusion(bf16[2048,512]{1,0:T(8,128)(2,1)} %get-tuple-element.6, bf16[1,2048,512]{2,1,0:T(8,128)(2,1)S(1)} %copy-done, bf16[2048,512]{1,0:T(8,128)(2,1)} %get-tuple-element.7, bf16[1,2048,512]{2,1,0:T(8,128)(2,1)S(1)} %copy-done.1), kind=kLoop, calls=%fused_computation.2 | loop fusion | flops 10485760 | bytes 12582912 | tf_op jit(solution)/shard_map/broadcast_in_dim | solution.py:460
  215.0 0.0 copy-done.2
  215.0 1.0 copy.14
Async XLA Ops:
  1.4 0.7 copy-start.3
  2.1 207.3 %copy-start = (bf16[1,2048,512]{2,1,0:T(8,128)(2,1)S(1)}, bf16[1,2048,512]{2,1,0:T(8,128)(2,1)}, u32[]{:S(2)}) copy-start(bf16[1,2048,512]{2,1,0:T(8,128)(2,1)} %param.8) | copy-start | bytes 6291460
  2.1 207.3 %copy-start.1 = (bf16[1,2048,512]{2,1,0:T(8,128)(2,1)S(1)}, bf16[1,2048,512]{2,1,0:T(8,128)(2,1)}, u32[]{:S(2)}) copy-start(bf16[1,2048,512]{2,1,0:T(8,128)(2,1)} %param.9) | copy-start | bytes 6291460
  209.4 5.6 %copy-start.2 = (f32[2,8,32,512]{3,2,1,0:T(8,128)S(1)}, f32[2,8,32,512]{3,2,1,0:T(8,128)}, u32[]{:S(2)}) copy-start(f32[2,8,32,512]{3,2,1,0:T(8,128)} %get-tuple-element.16) | copy-start | bytes 3145732
where the time goes:
time: 216 us
  Pallas kernels  207 us (96%)
  other arithmetic  5.6 us (3%)
  local copies, waits for them, and re-layouts  2.4 us (1%)
    pallas_call x1, Pallas kernels, sync(): pl.pallas_call(kernel, out_shape=(jax.ShapeDtypeStruct((D, COLS), jnp.bfl...  207 us
    broadcast_in_dim x1, other arithmetic, on_device(): apply(first, update_in)[None]  5.6 us

commit v1 on v0

v1 whole, which is shorter than its diff:
```python
import functools

import jax
import jax.numpy as jnp
from jax import lax
from jax.experimental import pallas as pl
from jax.experimental.pallas import tpu as pltpu
from jax.sharding import PartitionSpec as P

MU = 0.9
OUTER_LR = 0.7
MESH = pl.DeviceIdType.MESH

NX, NY, NZ, NC = 4, 4, 8, 2
GRID = 8
TOK = 256
TOKENS = TOK * NX
D = 2048
COLS = D // NX
PIECE = D // (NY * NZ * NC)
NPAIR = NZ // 2
PAIR = 2 * NC * PIECE
CHUNK = NY * PAIR
PEERS = [(2, 0), (2, 1), (1, 0), (1, 1), (3, 0), (3, 1), (0, 1)]
NP = len(PEERS)
ORDER = [2, 1, 3, 0]
AHEAD = 2
SCHEDULE = [
    ("forward_tokens", 0),
    ("forward_tokens", 1),
    ("product", 0, 0),
    ("forward_tokens", 2),
    ("product", 0, 1),
    ("forward_tokens", 3),
    ("product", 0, 2),
    ("forward_tokens", 4),
    ("product", 0, 3),
    ("activate",),
    ("forward_tokens", 5),
    ("gradient", 1, 0),
    ("product", 1, 0),
    ("forward_tokens", 6),
    ("hop", 1, 4, 0),
    ("hop", 1, 4, 1),
    ("gradient", 1, 1),
    ("product", 1, 1),
    ("forward_tokens", 7),
    ("gradient", 1, 2),
    ("hop", 1, 3, 0),
    ("hop", 1, 3, 1),
    ("product", 1, 2),
    ("gradient", 1, 3),
    ("product", 1, 3),
    ("slope",),
    ("gradient", 0, 0),
    ("gradient", 0, 1),
    ("hop", 1, -3, 0),
    ("hop", 1, -3, 1),
    ("gradient", 0, 2),
    ("gradient", 0, 3),
    ("hop", 1, 2, 0),
    ("hop", 1, 2, 1),
    ("hop", 1, -2, 0),
    ("hop", 1, -2, 1),
    ("hop", 1, 1, 0),
    ("hop", 1, -1, 0),
    ("hop", 0, 4, 0),
    ("hop", 0, 4, 1),
    ("hop", 1, 1, 1),
    ("hop", 1, -1, 1),
    ("own", 1, 0),
    ("hop", 0, 3, 0),
    ("hop", 0, 3, 1),
    ("own", 1, 1),
    ("hop", 0, -3, 0),
    ("hop", 0, -3, 1),
    ("give", 1, 0),
    ("spread", 1, -1, 0),
    ("spread", 1, 1, 0),
    ("hop", 0, 2, 0),
    ("spread", 1, 1, 1),
    ("give", 1, 1),
    ("hop", 0, 2, 1),
    ("hop", 0, -2, 0),
    ("spread", 1, -1, 1),
    ("give", 1, -1),
    ("hop", 0, -2, 1),
    ("spread", 1, -2, 0),
    ("spread", 1, 2, 0),
    ("hop", 0, 1, 0),
    ("spread", 1, 2, 1),
    ("give", 1, 2),
    ("hop", 0, 1, 1),
    ("hop", 0, -1, 0),
    ("spread", 1, -2, 1),
    ("give", 1, -2),
    ("hop", 0, -1, 1),
    ("spread", 1, -3, 0),
    ("spread", 1, 3, 0),
    ("spread", 1, 3, 1),
    ("give", 1, 3),
    ("own", 0, 0),
    ("spread", 1, -3, 1),
    ("give", 1, -3),
    ("own", 0, 1),
    ("give", 0, 0),
    ("spread", 0, -1, 0),
    ("give", 1, 4),
    ("spread", 0, 1, 0),
    ("spread", 0, -1, 1),
    ("give", 0, -1),
    ("spread", 0, 1, 1),
    ("give", 0, 1),
    ("spread", 0, -2, 0),
    ("spread", 0, 2, 0),
    ("spread", 0, -2, 1),
    ("give", 0, -2),
    ("spread", 0, 2, 1),
    ("give", 0, 2),
    ("spread", 0, -3, 0),
    ("spread", 0, 3, 0),
    ("spread", 0, -3, 1),
    ("give", 0, -3),
    ("spread", 0, 3, 1),
    ("give", 0, 3),
    ("give", 0, 4),
]
HOPS = [4, 3, 2, 1, -3, -2, -1]
READY = {4: 0, 3: 1, 2: 1, -3: 2, -2: 2, 1: 3, -1: 3, 0: 3}
PARTS = 2
WIDTH = COLS // PARTS


def contract_first(left, right):
    return lax.dot_general(
        left, right, (((0,), (0,)), ((), ())), preferred_element_type=jnp.float32
    )


class Body:
    def __init__(self, ins, outs, scratch):
        self.x_hbm, self.c_hbm, self.w1_hbm, self.w2_hbm, self.ch, self.chv, self.mom_hbm = ins
        self.f_hbm = outs[:2]
        self.nm_hbm = outs[2]
        for name, ref in scratch.items():
            setattr(self, name, ref)
        path = lax.axis_index("path")
        self.x = lax.axis_index("inner")
        self.y = lax.div(path, NZ * NC)
        self.z = lax.rem(lax.div(path, NC), NZ)
        self.c = lax.rem(path, NC)
        self.zp = lax.div(self.z, 2)

    def path_of(self, dy=0, dz=0, dc=0):
        y = lax.rem(self.y + (dy + NY), NY)
        z = lax.rem(self.z + (dz + NZ), NZ)
        c = lax.rem(self.c + (dc + NC), NC)
        return (y * NZ + z) * NC + c

    def dev(self, dy=0, dz=0, dc=0, dx=0):
        return (self.path_of(dy, dz, dc), lax.rem(self.x + (dx + NX), NX))

    def send(self, src, dst, ssem, rsem, dev):
        pltpu.make_async_remote_copy(
            src_ref=src, dst_ref=dst, send_sem=ssem, recv_sem=rsem, device_id=dev, device_id_type=MESH
        ).start()

    def wait(self, ref, sem):
        pltpu.make_async_copy(ref, ref, sem).wait()

    def barrier(self):
        bar = pltpu.get_barrier_semaphore()
        partners = [self.dev(dx=1), self.dev(dx=-1)]
        partners += [self.dev(dy=dy, dc=dc) for dy, dc in PEERS]
        partners += [self.dev(dz=1), self.dev(dz=-1)]
        for partner in partners:
            pl.semaphore_signal(bar, inc=1, device_id=partner, device_id_type=MESH)
        pl.semaphore_wait(bar, len(partners))

    def pair(self, i):
        return lax.rem(self.zp + ORDER[i], NPAIR)

    def load_local(self):
        for a, (hbm, whbm, wbuf) in enumerate(
            ((self.x_hbm, self.w1_hbm, self.W1), (self.c_hbm, self.w2_hbm, self.W2))
        ):
            for i in range(NPAIR):
                q = self.pair(i)

                def tokens(yy, _, a=a, i=i, q=q, hbm=hbm):
                    cols = pl.multiple_of(yy * (NPAIR * PAIR) + q * PAIR, PAIR)
                    pltpu.make_async_copy(
                        hbm.at[:, pl.ds(cols, PAIR)], self.T2[a].at[q, yy, self.x], self.lsem.at[a, i]
                    ).start()
                    return 0

                lax.fori_loop(0, NY, tokens, 0)
            for i in range(NPAIR):
                q = self.pair(i)

                def weights(yy, _, a=a, i=i, q=q, whbm=whbm, wbuf=wbuf):
                    rows = pl.multiple_of(yy * (NPAIR * PAIR) + q * PAIR, PAIR)
                    place = pl.multiple_of(yy * PAIR, PAIR)
                    pltpu.make_async_copy(
                        whbm.at[pl.ds(rows, PAIR)], wbuf.at[q, pl.ds(place, PAIR)], self.wsem.at[a, i]
                    ).start()
                    return 0

                lax.fori_loop(0, NY, weights, 0)
        pltpu.make_async_copy(self.mom_hbm, self.MOM, self.msem.at[0]).start()

    def send_tokens(self, n):
        a, i = divmod(n, NPAIR)
        own = self.T2[a].at[self.pair(i), :, self.x]
        self.wait(own, self.lsem.at[a, i])
        for k, dx in enumerate((1, -1)):
            self.send(own, own, self.tssem.at[a], self.trsem.at[a, i, k], self.dev(dx=dx))

    def forward_tokens(self, n):
        a, i = divmod(n, NPAIR)
        q = self.pair(i)
        for k, dx in enumerate((1, -1)):
            src = lax.rem(self.x + (NX - dx), NX)
            self.wait(self.T2[a].at[q, :, src], self.trsem.at[a, i, k])
            half = self.T2[a].at[q, pl.ds(k * (NY // 2), NY // 2), src]
            self.send(half, half, self.tssem.at[a], self.trsem.at[a, i, 2], self.dev(dx=dx))
        if n + AHEAD < 2 * NPAIR:
            self.send_tokens(n + AHEAD)

    def wait_tokens(self, n):
        if n in self.came:
            return
        self.came.add(n)
        a, i = divmod(n, NPAIR)
        q = self.pair(i)
        self.wait((self.W1, self.W2)[a].at[q], self.wsem.at[a, i])
        self.wait(self.T2[a].at[q, :, lax.rem(self.x + 2, NX)], self.trsem.at[a, i, 2])

    def product(self, a, i):
        self.wait_tokens(a * NPAIR + i)
        q = self.pair(i)
        wbuf = (self.W1, self.W2)[a]

        def one(h, _):
            rows = pl.ds(pl.multiple_of(h * 512, 512), 512)
            left = jnp.concatenate(
                [self.T2[a][q, yy, pl.ds(h * 2, 2)].reshape(512, PAIR) for yy in range(NY)], axis=1
            )
            part = jnp.dot(left, wbuf[q], preferred_element_type=jnp.float32)
            if i == 0:
                self.ACC[rows] = part
            else:
                self.ACC[rows] = self.ACC[rows] + part
            return 0

        lax.fori_loop(0, TOKENS // 512, one, 0)

    def activate(self):
        def one(h, _):
            rows = pl.ds(pl.multiple_of(h * 64, 64), 64)
            t = jnp.tanh(self.ACC[rows])
            self.TB[rows] = t.astype(jnp.bfloat16)
            self.SL[rows] = 1.0 - t * t
            return 0

        lax.fori_loop(0, TOKENS // 64, one, 0)

    def slope(self):
        def one(h, _):
            rows = pl.ds(pl.multiple_of(h * 64, 64), 64)
            self.DS[rows] = (self.ACC[rows] * self.SL[rows]).astype(jnp.bfloat16)
            return 0

        lax.fori_loop(0, TOKENS // 64, one, 0)

    def gradient(self, level, i):
        if level == 1:
            self.wait_tokens(NPAIR + i)
        q = self.pair(i)
        left = self.T2[level]
        right = (self.DS, self.TB)[level]

        def one(h, _):
            cols = jnp.concatenate([left[q, h * 2 + e].reshape(TOKENS, PAIR) for e in range(2)], axis=1)
            g = contract_first(cols, right[...]) * (1.0 / TOKENS**0.5)
            self.S[level, q, pl.ds(h * 2, 2)] = g.astype(jnp.bfloat16).reshape(2, 2, NC, PIECE, COLS)
            return 0

        lax.fori_loop(0, CHUNK // 256, one, 0)
        for k, (dy, dc) in enumerate(PEERS):
            yy = lax.rem(self.y + dy, NY)
            cc = lax.rem(self.c + dc, NC)
            self.send(
                self.S.at[level, q, yy, :, cc],
                self.R.at[level, k, pl.ds(q * 2, 2)],
                self.yssem.at[level],
                self.yrsem.at[level, i],
                self.dev(dy=dy, dc=dc),
            )

    def wait_gradient(self, level, i):
        if (level, i) in self.came:
            return
        self.came.add((level, i))
        q = self.pair(i)
        self.wait(self.R.at[level, :, pl.ds(q * 2, 2)], self.yrsem.at[level, i])

    def passed(self, level, d, h, use):
        t = lax.rem(self.z + (d + NZ), NZ)
        q = lax.div(t, 2)
        low = lax.rem(t, 2)
        ids = [self.ch[self.path_of() * 2 + level]]
        ids += [self.ch[self.path_of(dy=-dy, dc=-dc) * 2 + level] for dy, dc in PEERS]
        weight = [[jnp.where(i == m, 1.0, 0.0).astype(jnp.float32) for m in range(GRID)] for i in ids]

        def one(b, _):
            cols = pl.ds(pl.multiple_of(h * WIDTH + b * 128, 128), 128)
            parts = [self.S[level, q, self.y, low, self.c, :, cols].astype(jnp.float32)]
            parts += [self.R[level, k, t, :, cols].astype(jnp.float32) for k in range(NP)]
            for m in range(GRID):
                total = parts[0] * weight[0][m]
                for s in range(1, NP + 1):
                    total = total + parts[s] * weight[s][m]
                use(m, cols, pl.ds(pl.multiple_of(b * 128, 128), 128), total)
            return 0

        lax.fori_loop(0, WIDTH // 128, one, 0)

    def hop(self, level, d, h):
        self.wait_gradient(level, READY[d])
        slot = HOPS.index(d)
        up = d > 0
        k = abs(d)
        came = self.UP if up else self.DOWN
        if k < 4:
            self.wait(self.arriving(level, up, k, h), (self.usem if up else self.dsem).at[level, k, h])

        def use(m, cols, place, total):
            if k < 3 or k == 3 and (m < GRID // 2) == up:
                total = total + came[level, k, h, m, :, place].astype(jnp.float32)
            self.SB[level, slot, h, m, :, place] = total.astype(jnp.bfloat16)

        self.passed(level, d, h, use)
        sum_ref, ssem = self.SB.at[level, slot, h], self.zssem.at[level]
        if up:
            rows = pl.ds(0, GRID // 2 if k == 4 else GRID)
            self.send(sum_ref.at[rows], self.UP.at[level, k - 1, h, rows], ssem, self.usem.at[level, k - 1, h], self.dev(dz=1))
        if not up or k == 4:
            rows = pl.ds(GRID // 2, GRID // 2) if k == 4 else pl.ds(0, GRID)
            self.send(sum_ref.at[rows], self.DOWN.at[level, k - 1, h, rows], ssem, self.dsem.at[level, k - 1, h], self.dev(dz=-1))

    def arriving(self, level, up, k, h):
        half = GRID // 2
        buf = self.UP if up else self.DOWN
        if k == 3:
            return buf.at[level, 3, h, pl.ds(0 if up else half, half)]
        return buf.at[level, k, h]

    def counts(self):
        for level in range(2):
            ids = self.chv[:, level : level + 1]
            for m in range(GRID):
                n = jnp.sum(jnp.where(ids == m, 1.0, 0.0), axis=0, keepdims=True)
                self.INV[level, m] = jnp.broadcast_to(1.0 / jnp.maximum(n, 1.0), (8, 128))

    def own(self, level, h):
        self.wait_gradient(level, READY[0])
        if "momentum" not in self.came:
            self.came.add("momentum")
            self.wait(self.MOM, self.msem.at[0])
        self.wait(self.UP.at[level, 0, h], self.usem.at[level, 0, h])
        self.wait(self.DOWN.at[level, 0, h], self.dsem.at[level, 0, h])

        def use(m, cols, place, total):
            total = total + self.UP[level, 0, h, m, :, place].astype(jnp.float32)
            total = total + self.DOWN[level, 0, h, m, :, place].astype(jnp.float32)
            avg = total * self.INV[level, m, :1]
            mom = MU * self.MOM[level, m, :, cols] + avg
            self.NM[level, m, :, cols] = mom
            self.U[level][0][h, m, :, place] = (MU * mom + avg).astype(jnp.bfloat16)

        self.passed(level, 0, h, use)
        self.pass_on(level, 0, h)
        if h == PARTS - 1:
            pltpu.make_async_copy(self.NM.at[level], self.nm_hbm.at[level], self.msem.at[1 + level]).start()

    def pass_on(self, level, d, h):
        half = GRID // 2
        src = self.U[level][d % NZ].at[h]
        ssem = self.gssem.at[level]
        if d <= 0:
            to = self.U[level][(d - 1) % NZ].at[h]
            rows = pl.ds(0, half if d == -3 else GRID)
            self.send(src.at[rows], to.at[rows], ssem, self.gusem.at[level, 1 - d, h], self.dev(dz=1))
        if d >= 0:
            to = self.U[level][(d + 1) % NZ].at[h]
            rows = pl.ds(half, half) if d == 3 else pl.ds(0, GRID)
            self.send(src.at[rows], to.at[rows], ssem, self.gdsem.at[level, d + 1, h], self.dev(dz=-1))

    def spread(self, level, d, h):
        sem = self.gusem.at[level, -d, h] if d < 0 else self.gdsem.at[level, d, h]
        self.wait(self.U[level][d % NZ].at[h], sem)
        self.pass_on(level, d, h)

    def give(self, level, d):
        t = lax.rem(self.z + (d + NZ), NZ)
        rows = pl.ds(pl.multiple_of((self.y * NZ + t) * (NC * PIECE) + self.c * PIECE, PIECE), PIECE)
        buf = self.U[level][d % NZ]
        if d == 4:
            half = GRID // 2
            for h in range(PARTS):
                self.wait(buf.at[h, pl.ds(0, half)], self.gusem.at[level, 4, h])
                self.wait(buf.at[h, pl.ds(half, half)], self.gdsem.at[level, 4, h])
        dst = self.f_hbm[level].at[rows]
        for k, (dy, dc) in enumerate(PEERS + [(0, 0)]):
            m = self.ch[self.path_of(dy=dy, dc=dc) * 2 + level]
            src = self.SEL.at[level, d % NZ, k]
            for h in range(PARTS):
                src[:, h * WIDTH : (h + 1) * WIDTH] = buf[h, m]
            if k < NP:
                self.send(src, dst, self.fssem.at[level], self.frsem.at[level], self.dev(dy=dy, dc=dc))
            else:
                pltpu.make_async_copy(src, dst, self.flsem.at[level]).start()

    def finish(self):
        for level in range(2):
            self.wait(self.f_hbm[level].at[pl.ds(0, D // 8 * 7)], self.frsem.at[level])
            self.wait(self.f_hbm[level].at[pl.ds(0, D // 8)], self.flsem.at[level])
            self.wait(self.SEL.at[level, :, pl.ds(0, NP)], self.fssem.at[level])
            self.wait(self.SB.at[level], self.zssem.at[level])
            self.wait(self.SB.at[level], self.gssem.at[level])
            self.wait(self.R.at[level], self.yssem.at[level])
            self.wait(self.T2[level].at[pl.ds(0, 3)], self.tssem.at[level])
            self.wait(self.NM.at[level], self.msem.at[1 + level])

    def run(self):
        self.came = set()
        self.load_local()
        self.counts()
        self.barrier()
        for n in range(AHEAD):
            self.send_tokens(n)
        for step, *args in SCHEDULE:
            getattr(self, step)(*args)
        self.finish()


SCRATCH = dict(
    X=pltpu.VMEM((NPAIR, NY, NX, TOK, PAIR), jnp.bfloat16),
    C=pltpu.VMEM((NPAIR, NY, NX, TOK, PAIR), jnp.bfloat16),
    W1=pltpu.VMEM((NPAIR, CHUNK, COLS), jnp.bfloat16),
    W2=pltpu.VMEM((NPAIR, CHUNK, COLS), jnp.bfloat16),
    ACC=pltpu.VMEM((TOKENS, COLS), jnp.float32),
    SL=pltpu.VMEM((TOKENS, COLS), jnp.float32),
    TB=pltpu.VMEM((TOKENS, COLS), jnp.bfloat16),
    DS=pltpu.VMEM((TOKENS, COLS), jnp.bfloat16),
    S=pltpu.VMEM((2, NPAIR, NY, 2, NC, PIECE, COLS), jnp.bfloat16),
    R=pltpu.VMEM((2, NP, NZ, PIECE, COLS), jnp.bfloat16),
    SB=pltpu.VMEM((2, len(HOPS), PARTS, GRID, PIECE, WIDTH), jnp.bfloat16),
    UP=pltpu.VMEM((2, 4, PARTS, GRID, PIECE, WIDTH), jnp.bfloat16),
    DOWN=pltpu.VMEM((2, 4, PARTS, GRID, PIECE, WIDTH), jnp.bfloat16),
    MOM=pltpu.VMEM((2, GRID, PIECE, COLS), jnp.float32),
    NM=pltpu.VMEM((2, GRID, PIECE, COLS), jnp.float32),
    INV=pltpu.VMEM((2, GRID, 8, 128), jnp.float32),
    SEL=pltpu.VMEM((2, NZ, NP + 1, PIECE, COLS), jnp.bfloat16),
    lsem=pltpu.SemaphoreType.DMA((2, NPAIR)),
    wsem=pltpu.SemaphoreType.DMA((2, NPAIR)),
    tssem=pltpu.SemaphoreType.DMA((2,)),
    trsem=pltpu.SemaphoreType.DMA((2, NPAIR, 3)),
    yssem=pltpu.SemaphoreType.DMA((2,)),
    yrsem=pltpu.SemaphoreType.DMA((2, NPAIR)),
    zssem=pltpu.SemaphoreType.DMA((2,)),
    usem=pltpu.SemaphoreType.DMA((2, 4, PARTS)),
    dsem=pltpu.SemaphoreType.DMA((2, 4, PARTS)),
    gssem=pltpu.SemaphoreType.DMA((2,)),
    gusem=pltpu.SemaphoreType.DMA((2, 5, PARTS)),
    gdsem=pltpu.SemaphoreType.DMA((2, 5, PARTS)),
    fssem=pltpu.SemaphoreType.DMA((2,)),
    frsem=pltpu.SemaphoreType.DMA((2,)),
    flsem=pltpu.SemaphoreType.DMA((2,)),
    msem=pltpu.SemaphoreType.DMA((3,)),
)
UPDATES = [pltpu.VMEM((PARTS, GRID, PIECE, WIDTH), jnp.bfloat16)] * (2 * NZ)


def kernel(*refs):
    ins, outs, rest = refs[:7], refs[7:10], refs[10:]
    named = dict(zip(SCRATCH, rest))
    body = Body(ins, outs, named)
    updates = rest[len(SCRATCH) :]
    body.U = [updates[:NZ], updates[NZ:]]
    body.T2 = [body.X, body.C]
    body.run()


def sync(acts, cotan, first, second, choose, momentum):
    hbm = pl.BlockSpec(memory_space=pl.ANY)
    return pl.pallas_call(
        kernel,
        out_shape=(
            jax.ShapeDtypeStruct((D, COLS), jnp.bfloat16),
            jax.ShapeDtypeStruct((D, COLS), jnp.bfloat16),
            jax.ShapeDtypeStruct(momentum.shape, jnp.float32),
        ),
        in_specs=[hbm] * 4
        + [pl.BlockSpec(memory_space=pltpu.SMEM), pl.BlockSpec(memory_space=pltpu.VMEM), hbm],
        out_specs=[hbm] * 3,
        scratch_shapes=list(SCRATCH.values()) + UPDATES,
        compiler_params=pltpu.CompilerParams(
            collective_id=0, has_side_effects=True, vmem_limit_bytes=58 * 2**20
        ),
        cost_estimate=pl.CostEstimate(flops=8 * 10**9, bytes_accessed=2 * 10**7, transcendentals=0),
    )(acts, cotan, first, second, choose.reshape(-1), choose, momentum)


def on_device(acts, cotan, w_in, w_out_t, choose, momentum):
    first, second = w_in[0], w_out_t[0]
    update_in, update_out, new_momentum = sync(acts, cotan, first, second, choose, momentum)

    def apply(weight, update):
        return (weight.astype(jnp.float32) - OUTER_LR * update.astype(jnp.float32)).astype(jnp.bfloat16)

    return (apply(first, update_in)[None], apply(second, update_out)[None], new_momentum)


def solution(mesh):
    return jax.shard_map(
        on_device,
        mesh=mesh,
        in_specs=(
            P(("path", "inner"), None),
            P(("path", "inner"), None),
            P("path", None, "inner"),
            P("path", None, "inner"),
            P(),
            P(None, None, "path", "inner"),
        ),
        out_specs=(
            P("path", None, "inner"),
            P("path", None, "inner"),
            P(None, None, "path", "inner"),
        ),
        check_vma=False,
    )
```

time: 216 us -> 182 us (0.84)
  Pallas kernels: 207 us -> 174 us
    pallas_call x1, Pallas kernels: 207 us -> 174 us  [sync(): pl.pallas_call(kernel, out_shape=(jax.ShapeDtypeStruct((D, COLS), jnp.bfl...]
where the time goes in v1:
time: 182 us
  Pallas kernels  174 us (96%)
  other arithmetic  5.6 us (3%)
  local copies, waits for them, and re-layouts  2.4 us (1%)
    pallas_call x1, Pallas kernels, sync(): pl.pallas_call(kernel, out_shape=(jax.ShapeDtypeStruct((D, COLS), jnp.bfl...  174 us
    broadcast_in_dim x1, other arithmetic, on_device(): apply(first, update_in)[None]  5.6 us

profile of v1, /device:TPU:1, one launch (start us, length us, event | category | flops | bytes accessed | tf_op | source)
XLA Modules:
  0.0 182.3 jit_solution(12652121819355986117)
XLA Ops:
  0.6 0.8 copy.11.refs_5_
  1.4 0.0 copy-start.3
  1.4 0.7 reshape.9.refs_4_
  2.1 0.0 copy-done.3
  2.1 0.0 copy-start
  2.1 0.0 copy-start.1
  2.1 173.6 %shard_map.85 = (bf16[2048,512]{1,0:T(8,128)(2,1)}, bf16[2048,512]{1,0:T(8,128)(2,1)}, f32[2,8,32,512]{3,2,1,0:T(8,128)}) custom-call(bf16[256,2048]{1,0:T(8,128)(2,1)} %refs_0_.1, bf16[256,2048]{1,0:T(8,128)(2,1)} %refs_1_.1, bf16[2048,512]{1,0:T(8,128)(2,1)} %bitcast.8, bf16[2048,512]{1,0:T(8,128)(2,1)} %bitcast.9, s32[128]{0:T(128)} %reshape.9.refs_4_, ...), custom_call_target="tpu_custom_call" | custom-call | flops 8000000000 | bytes 20000000 | tf_op jit(solution)/shard_map/pallas_call | solution.py:498
  175.7 0.0 copy-done
  175.7 0.0 copy-done.1
  175.7 0.0 copy-start.2
  175.7 5.6 %fusion = (bf16[1,2048,512]{2,1,0:T(8,128)(2,1)}, bf16[1,2048,512]{2,1,0:T(8,128)(2,1)}) fusion(bf16[2048,512]{1,0:T(8,128)(2,1)} %get-tuple-element.6, bf16[1,2048,512]{2,1,0:T(8,128)(2,1)S(1)} %copy-done, bf16[2048,512]{1,0:T(8,128)(2,1)} %get-tuple-element.7, bf16[1,2048,512]{2,1,0:T(8,128)(2,1)S(1)} %copy-done.1), kind=kLoop, calls=%fused_computation.2 | loop fusion | flops 10485760 | bytes 12582912 | tf_op jit(solution)/shard_map/broadcast_in_dim | solution.py:523
  181.3 0.0 copy-done.2
  181.3 1.0 copy.14
Async XLA Ops:
  1.4 0.7 copy-start.3
  2.1 173.6 %copy-start = (bf16[1,2048,512]{2,1,0:T(8,128)(2,1)S(1)}, bf16[1,2048,512]{2,1,0:T(8,128)(2,1)}, u32[]{:S(2)}) copy-start(bf16[1,2048,512]{2,1,0:T(8,128)(2,1)} %param.8) | copy-start | bytes 6291460
  2.1 173.6 %copy-start.1 = (bf16[1,2048,512]{2,1,0:T(8,128)(2,1)S(1)}, bf16[1,2048,512]{2,1,0:T(8,128)(2,1)}, u32[]{:S(2)}) copy-start(bf16[1,2048,512]{2,1,0:T(8,128)(2,1)} %param.9) | copy-start | bytes 6291460
  175.7 5.6 %copy-start.2 = (f32[2,8,32,512]{3,2,1,0:T(8,128)S(1)}, f32[2,8,32,512]{3,2,1,0:T(8,128)}, u32[]{:S(2)}) copy-start(f32[2,8,32,512]{3,2,1,0:T(8,128)} %get-tuple-element.16) | copy-start | bytes 3145732

commit v2 on v1

--- a/solution.py
+++ b/solution.py
@@ -37,89 +37,105 @@
     ("product", 0, 3),
     ("activate",),
     ("forward_tokens", 5),
+    ("product", 1, 0),
     ("gradient", 1, 0),
-    ("product", 1, 0),
+    ("send_gradient", 1, 0, 1),
+    ("send_gradient", 1, 0, 0),
     ("forward_tokens", 6),
-    ("hop", 1, 4, 0),
     ("hop", 1, 4, 1),
     ("gradient", 1, 1),
+    ("send_gradient", 1, 1, 1),
     ("product", 1, 1),
+    ("send_gradient", 1, 1, 0),
+    ("hop", 1, 4, 0),
+    ("hop", 1, 3, 1),
     ("forward_tokens", 7),
+    ("hop", 1, 3, 0),
     ("gradient", 1, 2),
-    ("hop", 1, 3, 0),
-    ("hop", 1, 3, 1),
+    ("send_gradient", 1, 2, 0),
     ("product", 1, 2),
+    ("send_gradient", 1, 2, 1),
     ("gradient", 1, 3),
+    ("send_gradient", 1, 3, 0),
+    ("send_gradient", 1, 3, 1),
+    ("hop", 1, 2, 1),
+    ("hop", 1, -3, 0),
+    ("hop", 1, 2, 0),
     ("product", 1, 3),
     ("slope",),
+    ("gradient", 0, 1),
+    ("hop", 1, -3, 1),
     ("gradient", 0, 0),
-    ("gradient", 0, 1),
-    ("hop", 1, -3, 0),
-    ("hop", 1, -3, 1),
+    ("send_gradient", 0, 0, 1),
     ("gradient", 0, 2),
+    ("hop", 1, -2, 0),
+    ("send_gradient", 0, 0, 0),
+    ("send_gradient", 0, 2, 0),
+    ("send_gradient", 0, 1, 0),
+    ("hop", 1, 1, 0),
+    ("hop", 1, -2, 1),
+    ("send_gradient", 0, 2, 1),
     ("gradient", 0, 3),
-    ("hop", 1, 2, 0),
-    ("hop", 1, 2, 1),
-    ("hop", 1, -2, 0),
-    ("hop", 1, -2, 1),
-    ("hop", 1, 1, 0),
+    ("send_gradient", 0, 3, 0),
+    ("hop", 1, 1, 1),
     ("hop", 1, -1, 0),
+    ("hop", 0, 4, 1),
+    ("send_gradient", 0, 1, 1),
+    ("send_gradient", 0, 3, 1),
+    ("hop", 1, -1, 1),
     ("hop", 0, 4, 0),
-    ("hop", 0, 4, 1),
-    ("hop", 1, 1, 1),
-    ("hop", 1, -1, 1),
     ("own", 1, 0),
     ("hop", 0, 3, 0),
-    ("hop", 0, 3, 1),
     ("own", 1, 1),
+    ("give", 1, 0),
+    ("spread", 1, -1, 0),
     ("hop", 0, -3, 0),
     ("hop", 0, -3, 1),
-    ("give", 1, 0),
-    ("spread", 1, -1, 0),
+    ("hop", 0, 2, 0),
     ("spread", 1, 1, 0),
-    ("hop", 0, 2, 0),
+    ("spread", 1, -1, 1),
+    ("give", 1, -1),
+    ("hop", 0, 3, 1),
     ("spread", 1, 1, 1),
     ("give", 1, 1),
+    ("spread", 1, -2, 0),
+    ("hop", 0, -2, 0),
+    ("hop", 0, 1, 0),
+    ("hop", 0, -2, 1),
+    ("spread", 1, -2, 1),
+    ("give", 1, -2),
+    ("spread", 1, 2, 0),
     ("hop", 0, 2, 1),
-    ("hop", 0, -2, 0),
-    ("spread", 1, -1, 1),
-    ("give", 1, -1),
-    ("hop", 0, -2, 1),
-    ("spread", 1, -2, 0),
-    ("spread", 1, 2, 0),
-    ("hop", 0, 1, 0),
     ("spread", 1, 2, 1),
     ("give", 1, 2),
+    ("spread", 1, -3, 0),
+    ("hop", 0, -1, 0),
+    ("hop", 0, -1, 1),
+    ("spread", 1, -3, 1),
+    ("give", 1, -3),
+    ("spread", 1, 3, 0),
     ("hop", 0, 1, 1),
-    ("hop", 0, -1, 0),
-    ("spread", 1, -2, 1),
-    ("give", 1, -2),
-    ("hop", 0, -1, 1),
-    ("spread", 1, -3, 0),
-    ("spread", 1, 3, 0),
     ("spread", 1, 3, 1),
     ("give", 1, 3),
     ("own", 0, 0),
-    ("spread", 1, -3, 1),
-    ("give", 1, -3),
     ("own", 0, 1),
     ("give", 0, 0),
     ("spread", 0, -1, 0),
     ("give", 1, 4),
+    ("spread", 0, -1, 1),
     ("spread", 0, 1, 0),
-    ("spread", 0, -1, 1),
     ("give", 0, -1),
+    ("spread", 0, -2, 0),
     ("spread", 0, 1, 1),
     ("give", 0, 1),
-    ("spread", 0, -2, 0),
+    ("spread", 0, -2, 1),
     ("spread", 0, 2, 0),
-    ("spread", 0, -2, 1),
     ("give", 0, -2),
+    ("spread", 0, -3, 0),
     ("spread", 0, 2, 1),
     ("give", 0, 2),
-    ("spread", 0, -3, 0),
+    ("spread", 0, -3, 1),
     ("spread", 0, 3, 0),
-    ("spread", 0, -3, 1),
     ("give", 0, -3),
     ("spread", 0, 3, 1),
     ("give", 0, 3),
@@ -139,7 +155,7 @@
 
 class Body:
     def __init__(self, ins, outs, scratch):
-        self.x_hbm, self.c_hbm, self.w1_hbm, self.w2_hbm, self.ch, self.chv, self.mom_hbm = ins
+        self.x_hbm, self.c_hbm, self.w1_hbm, self.w2_hbm, self.ch, self.mom_hbm = ins
         self.f_hbm = outs[:2]
         self.nm_hbm = outs[2]
         for name, ref in scratch.items():
@@ -175,6 +191,7 @@
         partners += [self.dev(dz=1), self.dev(dz=-1)]
         for partner in partners:
             pl.semaphore_signal(bar, inc=1, device_id=partner, device_id_type=MESH)
+        self.load_local()
         pl.semaphore_wait(bar, len(partners))
 
     def pair(self, i):
@@ -283,51 +300,57 @@
         def one(h, _):
             cols = jnp.concatenate([left[q, h * 2 + e].reshape(TOKENS, PAIR) for e in range(2)], axis=1)
             g = contract_first(cols, right[...]) * (1.0 / TOKENS**0.5)
-            self.S[level, q, pl.ds(h * 2, 2)] = g.astype(jnp.bfloat16).reshape(2, 2, NC, PIECE, COLS)
+            g = g.astype(jnp.bfloat16).reshape(2, 2, NC, PIECE, COLS)
+            for part in range(PARTS):
+                self.S[level, part, q, pl.ds(h * 2, 2)] = g[..., part * WIDTH : (part + 1) * WIDTH]
             return 0
 
         lax.fori_loop(0, CHUNK // 256, one, 0)
+
+    def send_gradient(self, level, i, h):
+        q = self.pair(i)
         for k, (dy, dc) in enumerate(PEERS):
             yy = lax.rem(self.y + dy, NY)
             cc = lax.rem(self.c + dc, NC)
             self.send(
-                self.S.at[level, q, yy, :, cc],
-                self.R.at[level, k, pl.ds(q * 2, 2)],
+                self.S.at[level, h, q, yy, :, cc],
+                self.R.at[level, h, k, pl.ds(q * 2, 2)],
                 self.yssem.at[level],
-                self.yrsem.at[level, i],
+                self.yrsem.at[level, i, h],
                 self.dev(dy=dy, dc=dc),
             )
 
-    def wait_gradient(self, level, i):
-        if (level, i) in self.came:
+    def wait_gradient(self, level, i, h):
+        if (level, i, h) in self.came:
             return
-        self.came.add((level, i))
+        self.came.add((level, i, h))
         q = self.pair(i)
-        self.wait(self.R.at[level, :, pl.ds(q * 2, 2)], self.yrsem.at[level, i])
+        self.wait(self.R.at[level, h, :, pl.ds(q * 2, 2)], self.yrsem.at[level, i, h])
 
     def passed(self, level, d, h, use):
         t = lax.rem(self.z + (d + NZ), NZ)
         q = lax.div(t, 2)
         low = lax.rem(t, 2)
-        ids = [self.ch[self.path_of() * 2 + level]]
-        ids += [self.ch[self.path_of(dy=-dy, dc=-dc) * 2 + level] for dy, dc in PEERS]
+        ids = [self.ch[self.path_of(), level]]
+        ids += [self.ch[self.path_of(dy=-dy, dc=-dc), level] for dy, dc in PEERS]
         weight = [[jnp.where(i == m, 1.0, 0.0).astype(jnp.float32) for m in range(GRID)] for i in ids]
 
         def one(b, _):
             cols = pl.ds(pl.multiple_of(h * WIDTH + b * 128, 128), 128)
-            parts = [self.S[level, q, self.y, low, self.c, :, cols].astype(jnp.float32)]
-            parts += [self.R[level, k, t, :, cols].astype(jnp.float32) for k in range(NP)]
+            place = pl.ds(pl.multiple_of(b * 128, 128), 128)
+            parts = [self.S[level, h, q, self.y, low, self.c, :, place].astype(jnp.float32)]
+            parts += [self.R[level, h, k, t, :, place].astype(jnp.float32) for k in range(NP)]
             for m in range(GRID):
                 total = parts[0] * weight[0][m]
                 for s in range(1, NP + 1):
                     total = total + parts[s] * weight[s][m]
-                use(m, cols, pl.ds(pl.multiple_of(b * 128, 128), 128), total)
+                use(m, cols, place, total)
             return 0
 
         lax.fori_loop(0, WIDTH // 128, one, 0)
 
     def hop(self, level, d, h):
-        self.wait_gradient(level, READY[d])
+        self.wait_gradient(level, READY[d], h)
         slot = HOPS.index(d)
         up = d > 0
         k = abs(d)
@@ -358,13 +381,18 @@
 
     def counts(self):
         for level in range(2):
-            ids = self.chv[:, level : level + 1]
-            for m in range(GRID):
-                n = jnp.sum(jnp.where(ids == m, 1.0, 0.0), axis=0, keepdims=True)
-                self.INV[level, m] = jnp.broadcast_to(1.0 / jnp.maximum(n, 1.0), (8, 128))
+
+            def one(p, counts, level=level):
+                i = self.ch[p, level]
+                return tuple(n + jnp.where(i == m, 1, 0) for m, n in enumerate(counts))
+
+            counts = lax.fori_loop(0, NY * NZ * NC, one, (jnp.int32(0),) * GRID)
+            for m, n in enumerate(counts):
+                n = jnp.full((8, 128), n, jnp.int32).astype(jnp.float32)
+                self.INV[level, m] = 1.0 / jnp.maximum(n, 1.0)
 
     def own(self, level, h):
-        self.wait_gradient(level, READY[0])
+        self.wait_gradient(level, READY[0], h)
         if "momentum" not in self.came:
             self.came.add("momentum")
             self.wait(self.MOM, self.msem.at[0])
@@ -413,7 +441,7 @@
                 self.wait(buf.at[h, pl.ds(half, half)], self.gdsem.at[level, 4, h])
         dst = self.f_hbm[level].at[rows]
         for k, (dy, dc) in enumerate(PEERS + [(0, 0)]):
-            m = self.ch[self.path_of(dy=dy, dc=dc) * 2 + level]
+            m = self.ch[self.path_of(dy=dy, dc=dc), level]
             src = self.SEL.at[level, d % NZ, k]
             for h in range(PARTS):
                 src[:, h * WIDTH : (h + 1) * WIDTH] = buf[h, m]
@@ -435,11 +463,10 @@
 
     def run(self):
         self.came = set()
-        self.load_local()
-        self.counts()
         self.barrier()
         for n in range(AHEAD):
             self.send_tokens(n)
+        self.counts()
         for step, *args in SCHEDULE:
             getattr(self, step)(*args)
         self.finish()
@@ -454,8 +481,8 @@
     SL=pltpu.VMEM((TOKENS, COLS), jnp.float32),
     TB=pltpu.VMEM((TOKENS, COLS), jnp.bfloat16),
     DS=pltpu.VMEM((TOKENS, COLS), jnp.bfloat16),
-    S=pltpu.VMEM((2, NPAIR, NY, 2, NC, PIECE, COLS), jnp.bfloat16),
-    R=pltpu.VMEM((2, NP, NZ, PIECE, COLS), jnp.bfloat16),
+    S=pltpu.VMEM((2, PARTS, NPAIR, NY, 2, NC, PIECE, WIDTH), jnp.bfloat16),
+    R=pltpu.VMEM((2, PARTS, NP, NZ, PIECE, WIDTH), jnp.bfloat16),
     SB=pltpu.VMEM((2, len(HOPS), PARTS, GRID, PIECE, WIDTH), jnp.bfloat16),
     UP=pltpu.VMEM((2, 4, PARTS, GRID, PIECE, WIDTH), jnp.bfloat16),
     DOWN=pltpu.VMEM((2, 4, PARTS, GRID, PIECE, WIDTH), jnp.bfloat16),
@@ -468,7 +495,7 @@
     tssem=pltpu.SemaphoreType.DMA((2,)),
     trsem=pltpu.SemaphoreType.DMA((2, NPAIR, 3)),
     yssem=pltpu.SemaphoreType.DMA((2,)),
-    yrsem=pltpu.SemaphoreType.DMA((2, NPAIR)),
+    yrsem=pltpu.SemaphoreType.DMA((2, NPAIR, PARTS)),
     zssem=pltpu.SemaphoreType.DMA((2,)),
     usem=pltpu.SemaphoreType.DMA((2, 4, PARTS)),
     dsem=pltpu.SemaphoreType.DMA((2, 4, PARTS)),
@@ -484,7 +511,7 @@
 
 
 def kernel(*refs):
-    ins, outs, rest = refs[:7], refs[7:10], refs[10:]
+    ins, outs, rest = refs[:6], refs[6:9], refs[9:]
     named = dict(zip(SCRATCH, rest))
     body = Body(ins, outs, named)
     updates = rest[len(SCRATCH) :]
@@ -503,14 +530,14 @@
             jax.ShapeDtypeStruct(momentum.shape, jnp.float32),
         ),
         in_specs=[hbm] * 4
-        + [pl.BlockSpec(memory_space=pltpu.SMEM), pl.BlockSpec(memory_space=pltpu.VMEM), hbm],
+        + [pl.BlockSpec(memory_space=pltpu.SMEM), hbm],
         out_specs=[hbm] * 3,
         scratch_shapes=list(SCRATCH.values()) + UPDATES,
         compiler_params=pltpu.CompilerParams(
             collective_id=0, has_side_effects=True, vmem_limit_bytes=58 * 2**20
         ),
         cost_estimate=pl.CostEstimate(flops=8 * 10**9, bytes_accessed=2 * 10**7, transcendentals=0),
-    )(acts, cotan, first, second, choose.reshape(-1), choose, momentum)
+    )(acts, cotan, first, second, choose, momentum)
 
 
 def on_device(acts, cotan, w_in, w_out_t, choose, momentum):

time: 182 us -> 179 us (0.984)
  Pallas kernels: 174 us -> 171 us
    pallas_call x1, Pallas kernels: 174 us -> 171 us  [sync(): pl.pallas_call(kernel, out_shape=(jax.ShapeDtypeStruct((D, COLS), jnp.bfl...]
where the time goes in v2:
time: 179 us
  Pallas kernels  171 us (96%)
  other arithmetic  5.6 us (3%)
  local copies, waits for them, and re-layouts  2.36 us (1%)
    pallas_call x1, Pallas kernels, sync(): pl.pallas_call(kernel, out_shape=(jax.ShapeDtypeStruct((D, COLS), jnp.bfl...  171 us
    broadcast_in_dim x1, other arithmetic, on_device(): apply(first, update_in)[None]  5.6 us

profile of v2, /device:TPU:1, one launch (start us, length us, event | category | flops | bytes accessed | tf_op | source)
XLA Modules:
  0.0 179.2 jit_solution(2322833529238572573)
XLA Ops:
  0.6 1.4 copy.9.refs_4_
  2.0 0.0 copy-start
  2.0 0.0 copy-start.1
  2.0 170.6 %shard_map.85 = (bf16[2048,512]{1,0:T(8,128)(2,1)}, bf16[2048,512]{1,0:T(8,128)(2,1)}, f32[2,8,32,512]{3,2,1,0:T(8,128)}) custom-call(bf16[256,2048]{1,0:T(8,128)(2,1)} %refs_0_.1, bf16[256,2048]{1,0:T(8,128)(2,1)} %refs_1_.1, bf16[2048,512]{1,0:T(8,128)(2,1)} %bitcast.8, bf16[2048,512]{1,0:T(8,128)(2,1)} %bitcast.9, s32[64,2]{1,0:T(8,128)} %copy.9.refs_4_, ...), custom_call_target="tpu_custom_call" | custom-call | flops 8000000000 | bytes 20000000 | tf_op jit(solution)/shard_map/pallas_call | solution.py:525
  172.6 0.0 copy-done
  172.6 0.0 copy-done.1
  172.6 0.0 copy-start.2
  172.6 5.6 %fusion = (bf16[1,2048,512]{2,1,0:T(8,128)(2,1)}, bf16[1,2048,512]{2,1,0:T(8,128)(2,1)}) fusion(bf16[2048,512]{1,0:T(8,128)(2,1)} %get-tuple-element.6, bf16[1,2048,512]{2,1,0:T(8,128)(2,1)S(1)} %copy-done, bf16[2048,512]{1,0:T(8,128)(2,1)} %get-tuple-element.7, bf16[1,2048,512]{2,1,0:T(8,128)(2,1)S(1)} %copy-done.1), kind=kLoop, calls=%fused_computation.2 | loop fusion | flops 10485760 | bytes 12582912 | tf_op jit(solution)/shard_map/broadcast_in_dim | solution.py:550
  178.2 0.0 copy-done.2
  178.2 1.0 copy.11
Async XLA Ops:
  2.0 170.6 %copy-start = (bf16[1,2048,512]{2,1,0:T(8,128)(2,1)S(1)}, bf16[1,2048,512]{2,1,0:T(8,128)(2,1)}, u32[]{:S(2)}) copy-start(bf16[1,2048,512]{2,1,0:T(8,128)(2,1)} %param.8) | copy-start | bytes 6291460
  2.0 170.6 %copy-start.1 = (bf16[1,2048,512]{2,1,0:T(8,128)(2,1)S(1)}, bf16[1,2048,512]{2,1,0:T(8,128)(2,1)}, u32[]{:S(2)}) copy-start(bf16[1,2048,512]{2,1,0:T(8,128)(2,1)} %param.9) | copy-start | bytes 6291460
  172.6 5.6 %copy-start.2 = (f32[2,8,32,512]{3,2,1,0:T(8,128)S(1)}, f32[2,8,32,512]{3,2,1,0:T(8,128)}, u32[]{:S(2)}) copy-start(f32[2,8,32,512]{3,2,1,0:T(8,128)} %get-tuple-element.16) | copy-start | bytes 3145732

commit v3 on v2

--- a/solution.py
+++ b/solution.py
@@ -23,7 +23,7 @@
 CHUNK = NY * PAIR
 PEERS = [(2, 0), (2, 1), (1, 0), (1, 1), (3, 0), (3, 1), (0, 1)]
 NP = len(PEERS)
-ORDER = [2, 1, 3, 0]
+ORDER = [[2, 2], [1, 3], [3, 1], [0, 0]]
 AHEAD = 2
 SCHEDULE = [
     ("forward_tokens", 0),
@@ -39,110 +39,110 @@
     ("forward_tokens", 5),
     ("product", 1, 0),
     ("gradient", 1, 0),
+    ("send_gradient", 1, 0, 0),
     ("send_gradient", 1, 0, 1),
-    ("send_gradient", 1, 0, 0),
     ("forward_tokens", 6),
-    ("hop", 1, 4, 1),
+    ("hop", 1, 4, 0),
     ("gradient", 1, 1),
+    ("send_gradient", 1, 1, 0),
     ("send_gradient", 1, 1, 1),
     ("product", 1, 1),
-    ("send_gradient", 1, 1, 0),
-    ("hop", 1, 4, 0),
-    ("hop", 1, 3, 1),
+    ("hop", 1, 4, 1),
+    ("hop", 1, -3, 0),
     ("forward_tokens", 7),
     ("hop", 1, 3, 0),
+    ("hop", 1, 3, 1),
     ("gradient", 1, 2),
     ("send_gradient", 1, 2, 0),
+    ("send_gradient", 1, 2, 1),
+    ("hop", 1, -3, 1),
     ("product", 1, 2),
-    ("send_gradient", 1, 2, 1),
     ("gradient", 1, 3),
     ("send_gradient", 1, 3, 0),
     ("send_gradient", 1, 3, 1),
-    ("hop", 1, 2, 1),
-    ("hop", 1, -3, 0),
     ("hop", 1, 2, 0),
+    ("hop", 1, -2, 0),
     ("product", 1, 3),
     ("slope",),
+    ("gradient", 0, 2),
+    ("hop", 1, 2, 1),
+    ("hop", 1, -2, 1),
+    ("gradient", 0, 0),
+    ("send_gradient", 0, 0, 0),
+    ("send_gradient", 0, 0, 1),
+    ("hop", 1, 1, 0),
+    ("hop", 1, -1, 0),
     ("gradient", 0, 1),
-    ("hop", 1, -3, 1),
-    ("gradient", 0, 0),
-    ("send_gradient", 0, 0, 1),
-    ("gradient", 0, 2),
-    ("hop", 1, -2, 0),
-    ("send_gradient", 0, 0, 0),
+    ("send_gradient", 0, 1, 1),
+    ("send_gradient", 0, 1, 0),
+    ("hop", 1, 1, 1),
+    ("hop", 1, -1, 1),
+    ("gradient", 0, 3),
+    ("send_gradient", 0, 3, 1),
+    ("send_gradient", 0, 3, 0),
+    ("hop", 0, 4, 0),
     ("send_gradient", 0, 2, 0),
-    ("send_gradient", 0, 1, 0),
-    ("hop", 1, 1, 0),
-    ("hop", 1, -2, 1),
+    ("own", 1, 0),
     ("send_gradient", 0, 2, 1),
-    ("gradient", 0, 3),
-    ("send_gradient", 0, 3, 0),
-    ("hop", 1, 1, 1),
-    ("hop", 1, -1, 0),
     ("hop", 0, 4, 1),
-    ("send_gradient", 0, 1, 1),
-    ("send_gradient", 0, 3, 1),
-    ("hop", 1, -1, 1),
-    ("hop", 0, 4, 0),
-    ("own", 1, 0),
-    ("hop", 0, 3, 0),
     ("own", 1, 1),
     ("give", 1, 0),
     ("spread", 1, -1, 0),
+    ("spread", 1, 1, 0),
+    ("hop", 0, 3, 1),
+    ("hop", 0, 3, 0),
     ("hop", 0, -3, 0),
     ("hop", 0, -3, 1),
-    ("hop", 0, 2, 0),
-    ("spread", 1, 1, 0),
     ("spread", 1, -1, 1),
     ("give", 1, -1),
-    ("hop", 0, 3, 1),
     ("spread", 1, 1, 1),
     ("give", 1, 1),
     ("spread", 1, -2, 0),
+    ("spread", 1, 2, 0),
     ("hop", 0, -2, 0),
-    ("hop", 0, 1, 0),
+    ("hop", 0, 2, 0),
+    ("hop", 0, 2, 1),
     ("hop", 0, -2, 1),
     ("spread", 1, -2, 1),
     ("give", 1, -2),
-    ("spread", 1, 2, 0),
-    ("hop", 0, 2, 1),
     ("spread", 1, 2, 1),
     ("give", 1, 2),
     ("spread", 1, -3, 0),
+    ("spread", 1, 3, 0),
+    ("hop", 0, 1, 0),
     ("hop", 0, -1, 0),
+    ("hop", 0, 1, 1),
     ("hop", 0, -1, 1),
     ("spread", 1, -3, 1),
-    ("give", 1, -3),
-    ("spread", 1, 3, 0),
-    ("hop", 0, 1, 1),
     ("spread", 1, 3, 1),
     ("give", 1, 3),
+    ("give", 1, -3),
     ("own", 0, 0),
     ("own", 0, 1),
     ("give", 0, 0),
+    ("give", 1, 4),
     ("spread", 0, -1, 0),
-    ("give", 1, 4),
+    ("spread", 0, 1, 0),
     ("spread", 0, -1, 1),
-    ("spread", 0, 1, 0),
     ("give", 0, -1),
-    ("spread", 0, -2, 0),
     ("spread", 0, 1, 1),
     ("give", 0, 1),
+    ("spread", 0, -2, 0),
+    ("spread", 0, 2, 0),
     ("spread", 0, -2, 1),
-    ("spread", 0, 2, 0),
     ("give", 0, -2),
-    ("spread", 0, -3, 0),
     ("spread", 0, 2, 1),
     ("give", 0, 2),
+    ("spread", 0, -3, 0),
+    ("spread", 0, 3, 0),
     ("spread", 0, -3, 1),
-    ("spread", 0, 3, 0),
     ("give", 0, -3),
     ("spread", 0, 3, 1),
     ("give", 0, 3),
     ("give", 0, 4),
 ]
 HOPS = [4, 3, 2, 1, -3, -2, -1]
-READY = {4: 0, 3: 1, 2: 1, -3: 2, -2: 2, 1: 3, -1: 3, 0: 3}
+READY = {4: 0, 3: 1, -3: 1, 2: 2, -2: 2, 1: 3, -1: 3, 0: 3}
 PARTS = 2
 WIDTH = COLS // PARTS
 
@@ -195,7 +195,8 @@
         pl.semaphore_wait(bar, len(partners))
 
     def pair(self, i):
-        return lax.rem(self.zp + ORDER[i], NPAIR)
+        even, odd = ORDER[i]
+        return lax.rem(self.zp + even + (odd - even) * lax.rem(self.z, 2) + NPAIR, NPAIR)
 
     def load_local(self):
         for a, (hbm, whbm, wbuf) in enumerate(
@@ -320,19 +321,18 @@
                 self.dev(dy=dy, dc=dc),
             )
 
-    def wait_gradient(self, level, i, h):
-        if (level, i, h) in self.came:
-            return
-        self.came.add((level, i, h))
-        q = self.pair(i)
-        self.wait(self.R.at[level, h, :, pl.ds(q * 2, 2)], self.yrsem.at[level, i, h])
+    def wait_gradient(self, level, last, h):
+        for i in range(last + 1):
+            if (level, i, h) not in self.came:
+                self.came.add((level, i, h))
+                self.wait(self.R.at[level, h, :, pl.ds(self.pair(i) * 2, 2)], self.yrsem.at[level, i, h])
 
     def passed(self, level, d, h, use):
         t = lax.rem(self.z + (d + NZ), NZ)
         q = lax.div(t, 2)
         low = lax.rem(t, 2)
-        ids = [self.ch[self.path_of(), level]]
-        ids += [self.ch[self.path_of(dy=-dy, dc=-dc), level] for dy, dc in PEERS]
+        ids = [self.ch[level, self.path_of()]]
+        ids += [self.ch[level, self.path_of(dy=-dy, dc=-dc)] for dy, dc in PEERS]
         weight = [[jnp.where(i == m, 1.0, 0.0).astype(jnp.float32) for m in range(GRID)] for i in ids]
 
         def one(b, _):
@@ -383,7 +383,7 @@
         for level in range(2):
 
             def one(p, counts, level=level):
-                i = self.ch[p, level]
+                i = self.ch[level, p]
                 return tuple(n + jnp.where(i == m, 1, 0) for m, n in enumerate(counts))
 
             counts = lax.fori_loop(0, NY * NZ * NC, one, (jnp.int32(0),) * GRID)
@@ -441,7 +441,7 @@
                 self.wait(buf.at[h, pl.ds(half, half)], self.gdsem.at[level, 4, h])
         dst = self.f_hbm[level].at[rows]
         for k, (dy, dc) in enumerate(PEERS + [(0, 0)]):
-            m = self.ch[self.path_of(dy=dy, dc=dc), level]
+            m = self.ch[level, self.path_of(dy=dy, dc=dc)]
             src = self.SEL.at[level, d % NZ, k]
             for h in range(PARTS):
                 src[:, h * WIDTH : (h + 1) * WIDTH] = buf[h, m]
@@ -537,17 +537,71 @@
             collective_id=0, has_side_effects=True, vmem_limit_bytes=58 * 2**20
         ),
         cost_estimate=pl.CostEstimate(flops=8 * 10**9, bytes_accessed=2 * 10**7, transcendentals=0),
-    )(acts, cotan, first, second, choose, momentum)
+    )(acts, cotan, first, second, choose.T, momentum)
+
+
+BLOCKS = 4
+ROWS = D // BLOCKS
+
+
+def step_kernel(w1, w2, f1, f2, nm, o1, o2, nm_out, weight, update, result, mom, wsem, fsem, osem, msem):
+    pieces = [(level, b) for b in range(BLOCKS) for level in range(2)]
+
+    def load(level, b):
+        rows = pl.ds(b * ROWS, ROWS)
+        return (
+            pltpu.make_async_copy((w1, w2)[level].at[rows], weight.at[level, rows], wsem.at[level, b]),
+            pltpu.make_async_copy((f1, f2)[level].at[rows], update.at[level, rows], fsem.at[level, b]),
+        )
+
+    def store(level, b):
+        rows = pl.ds(b * ROWS, ROWS)
+        return pltpu.make_async_copy(result.at[level, rows], (o1, o2)[level].at[rows], osem.at[level, b])
+
+    for piece in pieces:
+        for copy in load(*piece):
+            copy.start()
+    pltpu.make_async_copy(nm, mom, msem).start()
+    for level, b in pieces:
+        for copy in load(level, b):
+            copy.wait()
+
+        def one(i, _, level=level, b=b):
+            rows = pl.ds(pl.multiple_of(b * ROWS + i * 64, 64), 64)
+            new = weight[level, rows].astype(jnp.float32) - OUTER_LR * update[level, rows].astype(jnp.float32)
+            result[level, rows] = new.astype(jnp.bfloat16)
+            return 0
+
+        lax.fori_loop(0, ROWS // 64, one, 0)
+        store(level, b).start()
+    pltpu.make_async_copy(nm, mom, msem).wait()
+    last = pltpu.make_async_copy(mom, nm_out, msem)
+    last.start()
+    for piece in pieces:
+        store(*piece).wait()
+    last.wait()
+
+
+def outer_step(first, second, update_in, update_out, new_momentum):
+    hbm = pl.BlockSpec(memory_space=pl.ANY)
+    whole = pltpu.VMEM((2, D, COLS), jnp.bfloat16)
+    sems = pltpu.SemaphoreType.DMA((2, BLOCKS))
+    return pl.pallas_call(
+        step_kernel,
+        out_shape=tuple(jax.ShapeDtypeStruct(a.shape, a.dtype) for a in (first, second, new_momentum)),
+        in_specs=[hbm] * 5,
+        out_specs=[hbm] * 3,
+        scratch_shapes=[whole, whole, whole, pltpu.VMEM(new_momentum.shape, jnp.float32), sems, sems, sems, pltpu.SemaphoreType.DMA],
+        compiler_params=pltpu.CompilerParams(vmem_limit_bytes=59 * 2**20),
+        cost_estimate=pl.CostEstimate(flops=4 * 10**6, bytes_accessed=14 * 2**20, transcendentals=0),
+    )(first, second, update_in, update_out, new_momentum)
 
 
 def on_device(acts, cotan, w_in, w_out_t, choose, momentum):
     first, second = w_in[0], w_out_t[0]
-    update_in, update_out, new_momentum = sync(acts, cotan, first, second, choose, momentum)
-
-    def apply(weight, update):
-        return (weight.astype(jnp.float32) - OUTER_LR * update.astype(jnp.float32)).astype(jnp.bfloat16)
-
-    return (apply(first, update_in)[None], apply(second, update_out)[None], new_momentum)
+    updates = sync(acts, cotan, first, second, choose, momentum)
+    new_in, new_out_t, new_momentum = outer_step(first, second, *updates)
+    return (new_in[None], new_out_t[None], new_momentum)
 
 
 def solution(mesh):

time: 179 us -> 173 us (0.966)
  other arithmetic: 5.6 us -> 0 us
  local copies, waits for them, and re-layouts: 2.36 us -> 0 us
    pallas_call x0 -> x1, Pallas kernels: none -> 5.88 us  [outer_step(): pl.pallas_call(step_kernel, out_shape=tuple((jax.ShapeDtypeStruct(a.shape...]
    broadcast_in_dim x1 -> x0, other arithmetic: 5.6 us -> none  [on_device(): apply(first, update_in)[None]]
    pallas_call x1, Pallas kernels: 171 us -> 167 us  [sync(): pl.pallas_call(kernel, out_shape=(jax.ShapeDtypeStruct((D, COLS), jnp.bfl...]
    unnamed x8 -> x0, local copies, waits for them, and re-layouts: 2.36 us -> none
where the time goes in v3:
time: 173 us
  Pallas kernels  172 us (99%)
    pallas_call x1, Pallas kernels, sync(): pl.pallas_call(kernel, out_shape=(jax.ShapeDtypeStruct((D, COLS), jnp.bfl...  167 us
    pallas_call x1, Pallas kernels, outer_step(): pl.pallas_call(step_kernel, out_shape=tuple((jax.ShapeDtypeStruct(a.shape...  5.88 us

profile of v3, /device:TPU:1, one launch (start us, length us, event | category | flops | bytes accessed | tf_op | source)
XLA Modules:
  0.0 173.1 jit_solution(750987528694157496)
XLA Ops:
  0.6 166.6 %shard_map.85 = (bf16[2048,512]{1,0:T(8,128)(2,1)}, bf16[2048,512]{1,0:T(8,128)(2,1)}, f32[2,8,32,512]{3,2,1,0:T(8,128)}) custom-call(bf16[256,2048]{1,0:T(8,128)(2,1)} %refs_0_.1, bf16[256,2048]{1,0:T(8,128)(2,1)} %refs_1_.1, bf16[2048,512]{1,0:T(8,128)(2,1)} %bitcast.5, bf16[2048,512]{1,0:T(8,128)(2,1)} %bitcast.7, s32[2,64]{1,0:T(2,128)} %bitcast.11, ...), custom_call_target="tpu_custom_call" | custom-call | flops 8000000000 | bytes 20000000 | tf_op jit(solution)/shard_map/pallas_call | solution.py:525
  167.2 5.9 %shard_map.86 = (bf16[2048,512]{1,0:T(8,128)(2,1)}, bf16[2048,512]{1,0:T(8,128)(2,1)}, f32[2,8,32,512]{3,2,1,0:T(8,128)}) custom-call(bf16[2048,512]{1,0:T(8,128)(2,1)} %bitcast.6, bf16[2048,512]{1,0:T(8,128)(2,1)} %bitcast.8, bf16[2048,512]{1,0:T(8,128)(2,1)} %get-tuple-element.9.f1, bf16[2048,512]{1,0:T(8,128)(2,1)} %get-tuple-element.10.f2, ...), custom_call_target="tpu_custom_call" | custom-call | flops 4000000 | bytes 14680064 | tf_op jit(solution)/shard_map/pallas_call | solution.py:589
